TPU v7x, 512 devices: a whole 4x8x8 slice. The times are simulated.
512 devices in a mesh: seq: 64 (over x, y, core), mp: 8 (over z).
Axes of the slice: x: 4, y: 8, z: 8, core: 2. Of those that a mesh axis runs over, the one named last changes fastest.
Arguments:
- token_ids: int32 [96, 2], replicated, may hold values from 0 to 25599
- prompt_lengths: int32 [6], replicated, may hold values from 1024 to 8192, as said below
- tail_lengths: int32 [96], replicated, may hold values from 32 to 256, as said below
- prompt_of: int32 [96], replicated, may hold values from 0 to 5, as said below
- page_table: int32 [96, 2], replicated, may hold values from 0 to 191, as said below
- prompt_keys: bfloat16 [49152, 6144], P('seq', 'mp'), may hold values from -240 to 240
- prompt_values: bfloat16 [49152, 6144], P('seq', 'mp'), may hold values from -12 to 12
- tail_keys: bfloat16 [24576, 6144], P('seq', 'mp'), may hold values from -240 to 240
- tail_values: bfloat16 [24576, 6144], P('seq', 'mp'), may hold values from -12 to 12
- norm_gain: bfloat16 [2, 7168], P(None, 'seq'), may hold values from 0.5 to 1.5
- norm_bias: bfloat16 [2, 7168], P(None, 'seq'), may hold values from -2 to 2
- qkv_weight: bfloat16 [7168, 3, 6144], P('seq', None, 'mp'), may hold values from -0.0625 to 0.0625
- qkv_bias: bfloat16 [3, 6144], P(None, 'mp'), may hold values from -2 to 2
- out_weight: bfloat16 [6144, 7168], P('mp', 'seq'), may hold values from -0.078125 to 0.078125
- out_bias: bfloat16 [7168], P('seq'), may hold values from -0.796875 to 0.796875
- embedding: bfloat16 [25600, 7168], P('mp', 'seq'), may hold values from -0.3984375 to 0.3984375
- score_weight: bfloat16 [7168], P('seq'), may hold values from -0.0625 to 0.0625
Outputs:
- hidden_states: bfloat16 [192, 7168], P(None, 'seq')
- score_values: float32 [96], replicated
- hidden_norms: float32 [192], replicated
- top_logits: float32 [96], replicated
Inputs may be any that keep to these rules, and one draw needn't show every extreme that they name: `prompt_lengths`: the longest prompt has exactly 8192 positions. `tail_lengths`: some continuation has exactly 256 tail tokens. `prompt_of`: each prompt is extended by 16 continuations or one more. `page_table`: all entries are distinct, so every pool page belongs to one continuation.
All inputs are finite; a program needn't handle non-finite values.
Results may differ from a plain program's by a relative error of at most 0.017.
The roundings to bfloat16 on the way count: a program that leaves them out, or rounds other values in their place, can miss the bound.
Values may be sent and summed in bfloat16 or wider, within the bound.
A program may use at most 128 MiB of HBM per device.

v0:
```python
import math
import jax
import jax.numpy as jnp
from jax import lax
from jax.sharding import PartitionSpec as P

D = 7168
HD = 128
PAGE = 128
epsilon = 1e-05
neg_fill = -1e30


def combine_parts(first, second):
    first_max, first_total, first_sum = first
    second_max, second_total, second_sum = second
    greatest = jnp.maximum(first_max, second_max)
    first_factor = jnp.exp(first_max - greatest)
    second_factor = jnp.exp(second_max - greatest)
    totals = first_total * first_factor + second_total * second_factor
    summed = first_sum * first_factor[..., None] + second_sum * second_factor[..., None]
    return (greatest, totals, summed)


def attend(queries, keys, values, valid, score_scale):
    scores = (
        jnp.einsum("cthe,nhe->chtn", queries, keys, preferred_element_type=jnp.float32)
        * score_scale
    )
    masked = valid[:, None, :, :]
    scores = jnp.where(masked, scores, neg_fill)
    greatest = jnp.max(scores, axis=-1)
    weights = jnp.where(masked, jnp.exp(scores - greatest[..., None]), 0.0)
    totals = jnp.sum(weights, axis=-1)
    summed = jnp.einsum(
        "chtn,nhe->chte", weights.astype(jnp.bfloat16), values, preferred_element_type=jnp.float32
    )
    return (greatest, totals, summed)


def per_device(
    token_ids,
    prompt_lengths,
    tail_lengths,
    prompt_of,
    page_table,
    prompt_keys,
    prompt_values,
    tail_keys,
    tail_values,
    norm_gain,
    norm_bias,
    qkv_weight,
    qkv_bias,
    out_weight,
    out_bias,
    embedding,
    score_weight,
):
    cont_count = token_ids.shape[0]
    row_count = 2 * cont_count
    vocab_local = embedding.shape[0]
    seq_index = lax.axis_index("seq")
    mp_index = lax.axis_index("mp")
    local_ids = token_ids.reshape(row_count) - mp_index * vocab_local
    inside = (local_ids >= 0) & (local_ids < vocab_local)
    picked = jnp.take(embedding, jnp.clip(local_ids, 0, vocab_local - 1), axis=0).astype(
        jnp.float32
    )
    picked = jnp.where(inside[:, None], picked, 0.0)
    inputs = lax.psum(picked, "mp").astype(jnp.bfloat16).astype(jnp.float32)
    input_sum, input_sq = lax.psum(
        (jnp.sum(inputs, axis=1), jnp.sum(inputs * inputs, axis=1)), "seq"
    )
    average = input_sum / D
    variance = input_sq / D - average * average
    gains = norm_gain.astype(jnp.float32)
    offsets = norm_bias.astype(jnp.float32)
    normed = (
        (inputs - average[:, None]) * lax.rsqrt(variance + epsilon)[:, None] * gains[0] + offsets[0]
    ).astype(jnp.bfloat16)
    partial_qkv = jnp.einsum("rd,dke->rke", normed, qkv_weight, preferred_element_type=jnp.float32)
    bias_rows = qkv_bias.astype(jnp.float32)
    qkv = (lax.psum(partial_qkv, "seq") + bias_rows).astype(jnp.bfloat16)
    head_local = qkv.shape[2] // HD
    queries = qkv[:, 0].reshape(cont_count, 2, head_local, HD)
    new_keys = qkv[:, 1].reshape(cont_count, 2, head_local, HD)
    new_values = qkv[:, 2].reshape(cont_count, 2, head_local, HD)
    score_scale = 1.0 / math.sqrt(HD)
    prompt_count = prompt_keys.shape[0]
    starts = jnp.cumsum(prompt_lengths) - prompt_lengths
    prompt_pick = (
        prompt_of[:, None] == jnp.arange(prompt_lengths.shape[0], dtype=jnp.int32)[None, :]
    ).astype(jnp.int32)
    begin = jnp.sum(prompt_pick * starts[None, :], axis=1)
    finish = begin + jnp.sum(prompt_pick * prompt_lengths[None, :], axis=1)
    position = seq_index * prompt_count + jnp.arange(prompt_count, dtype=jnp.int32)
    prompt_mask = (position[None, :] >= begin[:, None]) & (position[None, :] < finish[:, None])
    prompt_part = attend(
        queries,
        prompt_keys.reshape(prompt_count, head_local, HD),
        prompt_values.reshape(prompt_count, head_local, HD),
        prompt_mask[:, None, :],
        score_scale,
    )
    tail_count = tail_keys.shape[0]
    pages_local = tail_count // PAGE
    page_ids = seq_index * pages_local + jnp.arange(pages_local, dtype=jnp.int32)
    owned = page_table[:, :, None] == page_ids[None, None, :]
    offsets_tail = (
        jnp.arange(2, dtype=jnp.int32)[:, None] * PAGE + jnp.arange(PAGE, dtype=jnp.int32)[None, :]
    )
    filled = offsets_tail[None, :, :] < tail_lengths[:, None, None]
    tail_mask = jnp.any(owned[:, :, :, None] & filled[:, :, None, :], axis=1).reshape(
        cont_count, tail_count
    )
    tail_part = attend(
        queries,
        tail_keys.reshape(tail_count, head_local, HD),
        tail_values.reshape(tail_count, head_local, HD),
        tail_mask[:, None, :],
        score_scale,
    )
    local_part = combine_parts(prompt_part, tail_part)
    greatest = lax.pmax(local_part[0], "seq")
    factor = jnp.exp(local_part[0] - greatest)
    totals, summed = lax.psum((local_part[1] * factor, local_part[2] * factor[..., None]), "seq")
    merged = (greatest, totals, summed)
    self_scores = (
        jnp.einsum("cthe,cshe->chts", queries, new_keys, preferred_element_type=jnp.float32)
        * score_scale
    )
    causal = (jnp.arange(2, dtype=jnp.int32)[:, None] >= jnp.arange(2, dtype=jnp.int32)[None, :])[
        None, None, :, :
    ]
    self_scores = jnp.where(causal, self_scores, neg_fill)
    self_max = jnp.max(self_scores, axis=-1)
    self_weights = jnp.where(causal, jnp.exp(self_scores - self_max[..., None]), 0.0)
    self_total = jnp.sum(self_weights, axis=-1)
    self_sum = jnp.einsum(
        "chts,cshe->chte",
        self_weights.astype(jnp.bfloat16),
        new_values,
        preferred_element_type=jnp.float32,
    )
    greatest, totals, summed = combine_parts(merged, (self_max, self_total, self_sum))
    attended = (
        (summed / totals[..., None])
        .transpose(0, 2, 1, 3)
        .reshape(row_count, head_local * HD)
        .astype(jnp.bfloat16)
    )
    projected = jnp.dot(attended, out_weight, preferred_element_type=jnp.float32)
    hidden = inputs + lax.psum(projected, "mp") + out_bias.astype(jnp.float32)
    hidden_sum, hidden_sq = lax.psum(
        (jnp.sum(hidden, axis=1), jnp.sum(hidden * hidden, axis=1)), "seq"
    )
    hidden_norms = jnp.sqrt(hidden_sq / D)
    last_rows = hidden.reshape(cont_count, 2, hidden.shape[1])[:, 1]
    last_average = hidden_sum.reshape(cont_count, 2)[:, 1] / D
    last_variance = hidden_sq.reshape(cont_count, 2)[:, 1] / D - last_average * last_average
    final = (
        (last_rows - last_average[:, None]) * lax.rsqrt(last_variance + epsilon)[:, None] * gains[1]
        + offsets[1]
    ).astype(jnp.bfloat16)
    score_values = lax.psum(jnp.dot(final, score_weight, preferred_element_type=jnp.float32), "seq")
    logit_share = lax.psum_scatter(
        lax.dot_general(
            embedding, final, (((1,), (1,)), ((), ())), preferred_element_type=jnp.float32
        ),
        "seq",
        scatter_dimension=0,
        tiled=True,
    )
    top_logits = lax.pmax(jnp.max(logit_share, axis=0), ("seq", "mp"))
    return (hidden.astype(jnp.bfloat16), score_values, hidden_norms, top_logits)


def solution(mesh):
    return jax.shard_map(
        per_device,
        mesh=mesh,
        in_specs=(
            P(),
            P(),
            P(),
            P(),
            P(),
            P("seq", "mp"),
            P("seq", "mp"),
            P("seq", "mp"),
            P("seq", "mp"),
            P(None, "seq"),
            P(None, "seq"),
            P("seq", None, "mp"),
            P(None, "mp"),
            P("mp", "seq"),
            P("seq"),
            P("mp", "seq"),
            P("seq"),
        ),
        out_specs=(P(None, "seq"), P(), P(), P()),
        check_vma=False,
    )
```

profile of v0, /device:TPU:1, one launch (start us, length us, event | category | flops | bytes accessed | tf_op | source)
XLA Modules:
  0.0 1449.8 jit_solution(1172715131099909362)
XLA Ops:
  9.1 1.5 copy.159
  10.9 0.8 gather_fusion
  11.8 30.5 %psum.70 = bf16[192,112]{1,0:T(8,128)(2,1)S(1)} all-reduce(f32[192,112]{1,0:T(8,128)S(1)} %convert_select_fusion), channel_id=1, replica_groups=mesh['seq'=64,'mp'=8] {'mp'}, use_global_device_ids=true, to_apply=%region_0.1 | all-reduce | flops 21504 | bytes 129024 | tf_op jit(solution)/shard_map/psum | solution.py:71
  43.1 131.9 %all-reduce.2 = (f32[192]{0:T(256)S(1)}, f32[192]{0:T(256)S(1)}) all-reduce(f32[192]{0:T(256)S(1)} %get-tuple-element.9, f32[192]{0:T(256)S(1)} %get-tuple-element.8), channel_id=1, replica_groups=mesh['seq'=64,'mp'=8] {'seq'}, use_global_device_ids=true, to_apply=%region_7.8 | all-reduce | flops 384 | bytes 3072 | tf_op jit(solution)/shard_map/psum | solution.py:72
  175.0 1.7 fusion.51
  176.9 1.1 copy.166
  178.8 2.4 copy.163
  181.2 1.1 copy.169
  183.5 178.7 %all-reduce.8.cloned.1.call-done = f32[192,3,768]{2,0,1:T(8,128)} async-done(((f32[192,3,768]{2,0,1:T(8,128)}), f32[192,3,768]{2,0,1:T(8,128)}) %all-reduce.8.cloned.1.call-update) | async-done | bytes 1769488 | tf_op jit(solution)/shard_map/psum | solution.py:84
  362.2 1.6 add_convert_fusion
  367.1 1.8 bitcast_reduce_fusion.1
  368.9 1.3 fusion.16
  370.2 0.9 bitcast_reduce_fusion
  371.7 1.1 copy-done.1
  372.9 1.8 fusion.2
  374.7 128.4 %pmax.14 = f32[96,6,2]{0,2,1:T(2,128)} all-reduce(f32[96,6,2]{0,2,1:T(2,128)} %max.21), channel_id=1, replica_groups=mesh['seq'=64,'mp'=8] {'seq'}, use_global_device_ids=true, to_apply=%region_12.13 | all-reduce | flops 1152 | bytes 9216 | tf_op jit(solution)/shard_map/pmax | solution.py:125
  503.0 1.4 add_multiply_fusion
  504.4 130.1 %psum.75 = f32[96,6,2]{0,2,1:T(2,128)} all-reduce(f32[96,6,2]{0,2,1:T(2,128)} %get-tuple-element.22), channel_id=1, replica_groups=mesh['seq'=64,'mp'=8] {'seq'}, use_global_device_ids=true, to_apply=%region_17.18 | all-reduce | flops 1152 | bytes 9216 | tf_op jit(solution)/shard_map/psum | solution.py:127
  634.5 3.3 fusion.18
  638.0 1.7 fusion.15
  641.4 184.1 %all-reduce.10.cloned.1.call-done = f32[96,6,2,128]{3,0,2,1:T(8,128)} async-done(((f32[96,6,2,128]{3,0,2,1:T(8,128)}), f32[96,6,2,128]{3,0,2,1:T(8,128)}) %all-reduce.10.cloned.1.call-update) | async-done | bytes 589840 | tf_op jit(solution)/shard_map/psum | solution.py:127
  825.5 1.7 fusion.34
  827.4 0.9 fusion.31
  828.4 74.0 %all-reduce.12.cloned.1.call-done = f32[192,112]{1,0:T(8,128)} async-done(((f32[192,112]{1,0:T(8,128)}), f32[192,112]{1,0:T(8,128)}) %all-reduce.12.cloned.1.call-update) | async-done | bytes 86032 | tf_op jit(solution)/shard_map/psum | solution.py:154
  902.4 1.0 fusion.72
  903.6 245.9 %all-reduce.1 = (f32[96,2]{1,0:T(8,128)S(1)}, f32[192]{0:T(256)S(1)}) all-reduce(f32[96,2]{1,0:T(8,128)S(1)} %reshape.242, f32[192]{0:T(256)S(1)} %get-tuple-element.5), channel_id=1, replica_groups=mesh['seq'=64,'mp'=8] {'seq'}, use_global_device_ids=true, to_apply=%region_21.22 | all-reduce | flops 384 | bytes 3072 | tf_op jit(solution)/shard_map/psum | solution.py:155
  1150.0 1.4 convolution_bitcast_fusion
  1151.4 1.3 dynamic-slice
  1154.1 129.6 %psum.79 = f32[96]{0:T(128)} all-reduce(f32[96]{0:T(128)S(1)} %convolution_bitcast_fusion.2), channel_id=1, replica_groups=mesh['seq'=64,'mp'=8] {'seq'}, use_global_device_ids=true, to_apply=%region_24.25 | all-reduce | flops 96 | bytes 768 | tf_op jit(solution)/shard_map/psum | solution.py:166
  1284.3 58.6 %all-reduce.14.cloned.1.call-done = f32[3200,96]{0,1:T(8,128)} async-done(((f32[3200,96]{0,1:T(8,128)}), f32[3200,96]{0,1:T(8,128)}) %all-reduce.14.cloned.1.call-update) | async-done | bytes 1228816
  1342.8 1.1 dynamic-slice_reduce_fusion
  1343.9 99.3 %pmax.15 = f32[96]{0:T(128)} all-reduce(f32[96]{0:T(128)S(1)} %dynamic-slice_reduce_fusion), channel_id=1, replica_groups=mesh['seq'=64,'mp'=8] {'seq','mp'}, use_global_device_ids=true, to_apply=%region_27.28 | all-reduce | flops 96 | bytes 768 | tf_op jit(solution)/shard_map/pmax | solution.py:175
  (132 shorter events, 12.9 us)
Async XLA Ops:
  7.2 167.8 %copy-start = (bf16[112,3,768]{2,0,1:T(8,128)(2,1)S(1)}, bf16[112,3,768]{2,0,1:T(8,128)(2,1)}, u32[]{:S(2)}) copy-start(bf16[112,3,768]{2,0,1:T(8,128)(2,1)} %param.28) | copy-start | bytes 1548292
  7.2 35.1 %copy-start.32 = (bf16[2,112]{1,0:T(2,128)(2,1)S(1)}, bf16[2,112]{1,0:T(2,128)(2,1)}, u32[]{:S(2)}) copy-start(bf16[2,112]{1,0:T(2,128)(2,1)} %param.27) | copy-start | bytes 1348
  7.2 35.2 %copy-start.33 = (bf16[2,112]{1,0:T(2,128)(2,1)S(1)}, bf16[2,112]{1,0:T(2,128)(2,1)}, u32[]{:S(2)}) copy-start(bf16[2,112]{1,0:T(2,128)(2,1)} %param.26) | copy-start | bytes 1348
  7.2 355.0 %all-reduce.8.cloned.1.call-start = ((), (), s32[]{:S(2)}) async-start(), calls=%async_computation | async-start | bytes 3538944 | tf_op jit(solution)/shard_map/psum | solution.py:84
  42.3 134.4 %copy-start.8 = (bf16[192,112]{1,0:T(8,128)(2,1)}, bf16[192,112]{1,0:T(8,128)(2,1)S(1)}, u32[]{:S(2)}) copy-start(bf16[192,112]{1,0:T(8,128)(2,1)S(1)} %psum.70) | copy-start | bytes 129028
  176.7 648.8 %all-reduce.10.cloned.1.call-start = ((), (), s32[]{:S(2)}) async-start(), calls=%async_computation.1 | async-start | bytes 1179648 | tf_op jit(solution)/shard_map/psum | solution.py:127
  178.2 3.1 copy-start.11
  178.8 3.5 copy-start.27
  178.8 3.6 copy-start.29
  178.8 3.7 copy-start.30
  366.3 2.6 copy-start.13
  367.1 3.1 copy-start.4
  372.9 261.7 %copy-start.6 = (bf16[768,768]{0,1:T(8,128)(2,1)S(1)}, bf16[768,768]{0,1:T(8,128)(2,1)}, u32[]{:S(2)}) copy-start(bf16[768,768]{0,1:T(8,128)(2,1)} %copy.163) | copy-start | bytes 3538948
  634.5 3.3 copy-start.12
  634.5 3.3 copy-start.14
  634.5 3.3 copy-start.23
  634.5 3.4 copy-start.24
  637.9 2.0 copy-start.19
  637.9 2.0 copy-start.17
  637.9 2.0 copy-start.18
  637.9 2.0 copy-start.20
  637.9 2.0 copy-start.21
  637.9 2.3 copy-start.7
  639.6 262.7 %all-reduce.12.cloned.1.call-start = ((), (), s32[]{:S(2)}) async-start(), calls=%async_computation.2 | async-start | bytes 196608 | tf_op jit(solution)/shard_map/psum | solution.py:154
  640.6 186.8 %copy-start.15 = (bf16[768,112]{0,1:T(8,128)(2,1)S(1)}, bf16[768,112]{0,1:T(8,128)(2,1)}, u32[]{:S(2)}) copy-start(bf16[768,112]{0,1:T(8,128)(2,1)} %param.30) | copy-start | bytes 516100
  641.3 187.0 %copy-start.34 = (bf16[112]{0:T(256)(128)(2,1)S(1)}, bf16[112]{0:T(256)(128)(2,1)}, u32[]{:S(2)}) copy-start(bf16[112]{0:T(256)(128)(2,1)} %param.31) | copy-start | bytes 676
  641.3 261.0 %copy-start.9 = (bf16[192,112]{1,0:T(8,128)(2,1)S(1)}, bf16[192,112]{1,0:T(8,128)(2,1)}, u32[]{:S(2)}) copy-start(bf16[192,112]{1,0:T(8,128)(2,1)} %copy-done.8) | copy-start | bytes 129028
  641.4 508.5 %copy-start.25 = (f32[112]{0:T(128)S(1)}, f32[112]{0:T(128)}, u32[]{:S(2)}) copy-start(f32[112]{0:T(128)} %get-tuple-element.31) | copy-start | bytes 1348
  641.4 508.5 %copy-start.26 = (f32[112]{0:T(128)S(1)}, f32[112]{0:T(128)}, u32[]{:S(2)}) copy-start(f32[112]{0:T(128)} %get-tuple-element.40) | copy-start | bytes 1348
  825.5 324.5 %copy-start.2 = (bf16[3200,112]{0,1:T(8,128)(2,1)S(1)}, bf16[3200,112]{0,1:T(8,128)(2,1)}, u32[]{:S(2)}) copy-start(bf16[3200,112]{0,1:T(8,128)(2,1)} %param.32) | copy-start | bytes 2150404
  828.3 514.5 %all-reduce.14.cloned.1.call-start = ((), (), s32[]{:S(2)}) async-start(), calls=%async_computation.3 | async-start | bytes 2457600
  1149.7 4.3 copy-start.31
  (7 other events, 10.7 us)
Sparse Core Ops, SparseCore 0:
  176.8 185.3 all-reduce.7
  639.8 185.7 all-reduce.9
  828.4 73.9 all-reduce.11
  1151.5 191.2 all-reduce.13
where the time goes:
time: 1450 us
  blocking collectives  896 us (62%)
  waiting for transfers between devices  495 us (34%)
  other arithmetic  15.3 us (1%)
  between operations  15 us (1%)
  local copies, waits for them, and re-layouts  14.7 us (1%)
    psum x1, blocking collectives, per_device(): lax.psum((jnp.sum(hidden, axis=1), jnp.sum(hidden * hidden, axis=1)), 'seq')  246 us
    psum x1, waiting for transfers between devices, per_device(): lax.psum((local_part[1] * factor, local_part[2] * factor[..., None]), 'seq')  184 us
    psum x1, waiting for transfers between devices, per_device(): qkv = (lax.psum(partial_qkv, 'seq') + bias_rows).astype(jnp.bfloat16)  179 us
    psum x1, blocking collectives, per_device(): lax.psum((jnp.sum(inputs, axis=1), jnp.sum(inputs * inputs, axis=1)), 'seq')  132 us
    psum x1, blocking collectives, per_device(): lax.psum((local_part[1] * factor, local_part[2] * factor[..., None]), 'seq')  130 us
    psum x1, blocking collectives, per_device(): lax.psum(jnp.dot(final, score_weight, preferred_element_type=jnp.float32)...  130 us
    pmax x1, blocking collectives, per_device(): greatest = lax.pmax(local_part[0], 'seq')  128 us
    pmax x1, blocking collectives, per_device(): top_logits = lax.pmax(jnp.max(logit_share, axis=0), ('seq', 'mp'))  99.3 us
  transfers between devices with their start and end apart: 4, of which 4 were waited for; matrix products, arithmetic and copies ran while one was open for 1% of the time, Pallas kernels for 0%

commit v1 on v0

--- a/solution.py
+++ b/solution.py
@@ -163,7 +163,9 @@
         (last_rows - last_average[:, None]) * lax.rsqrt(last_variance + epsilon)[:, None] * gains[1]
         + offsets[1]
     ).astype(jnp.bfloat16)
-    score_values = lax.psum(jnp.dot(final, score_weight, preferred_element_type=jnp.float32), "seq")
+    x = jnp.dot(final, score_weight, preferred_element_type=jnp.float32)
+    pieces = lax.all_gather(x, "seq")
+    score_values = jnp.sum(pieces, axis=0)
     logit_share = lax.psum_scatter(
         lax.dot_general(
             embedding, final, (((1,), (1,)), ((), ())), preferred_element_type=jnp.float32

time: 1450 us -> 1510 us (1.041)
  blocking collectives: 896 us -> 1010 us
  waiting for transfers between devices: 495 us -> 437 us
    unnamed x0 -> x1, blocking collectives: none -> 246 us
    psum x1 -> x0, blocking collectives: 130 us -> none  [per_device(): lax.psum(jnp.dot(final, score_weight, preferred_element_type=jnp.float32)...]
    unnamed x5, waiting for transfers between devices: 58.6 us -> 0.07 us
  transfers between devices with their start and end apart: 4 -> 4, of which waited for: 4 -> 3; matrix products, arithmetic and copies ran while one was open for 1% -> 1% of each run, Pallas kernels for 0% -> 0%
where the time goes in v1:
time: 1510 us
  blocking collectives  1010 us (67%)
  waiting for transfers between devices  437 us (29%)
  other arithmetic  15.9 us (1%)
  between operations  15.7 us (1%)
    unnamed x1, blocking collectives  246 us
    psum x1, blocking collectives, per_device(): lax.psum((jnp.sum(hidden, axis=1), jnp.sum(hidden * hidden, axis=1)), 'seq')  246 us
    psum x1, waiting for transfers between devices, per_device(): lax.psum((local_part[1] * factor, local_part[2] * factor[..., None]), 'seq')  184 us
    psum x1, waiting for transfers between devices, per_device(): qkv = (lax.psum(partial_qkv, 'seq') + bias_rows).astype(jnp.bfloat16)  179 us
    psum x1, blocking collectives, per_device(): lax.psum((jnp.sum(inputs, axis=1), jnp.sum(inputs * inputs, axis=1)), 'seq')  132 us
    psum x1, blocking collectives, per_device(): lax.psum((local_part[1] * factor, local_part[2] * factor[..., None]), 'seq')  130 us
    pmax x1, blocking collectives, per_device(): greatest = lax.pmax(local_part[0], 'seq')  128 us
    pmax x1, blocking collectives, per_device(): top_logits = lax.pmax(jnp.max(logit_share, axis=0), ('seq', 'mp'))  97.9 us
  transfers between devices with their start and end apart: 4, of which 3 were waited for; matrix products, arithmetic and copies ran while one was open for 1% of the time, Pallas kernels for 0%

profile of v1, /device:TPU:1, one launch (start us, length us, event | category | flops | bytes accessed | tf_op | source)
XLA Modules:
  0.0 1507.3 jit_solution(12532436178633487252)
XLA Ops:
  9.1 1.5 copy.159
  10.9 0.8 gather_fusion
  11.8 30.5 %psum.63 = bf16[192,112]{1,0:T(8,128)(2,1)S(1)} all-reduce(f32[192,112]{1,0:T(8,128)S(1)} %convert_select_fusion), channel_id=1, replica_groups=mesh['seq'=64,'mp'=8] {'mp'}, use_global_device_ids=true, to_apply=%region_0.1 | all-reduce | flops 21504 | bytes 129024 | tf_op jit(solution)/shard_map/psum | solution.py:71
  43.1 131.9 %all-reduce.3 = (f32[192]{0:T(256)S(1)}, f32[192]{0:T(256)S(1)}) all-reduce(f32[192]{0:T(256)S(1)} %get-tuple-element.9, f32[192]{0:T(256)S(1)} %get-tuple-element.8), channel_id=1, replica_groups=mesh['seq'=64,'mp'=8] {'seq'}, use_global_device_ids=true, to_apply=%region_7.8 | all-reduce | flops 384 | bytes 3072 | tf_op jit(solution)/shard_map/psum | solution.py:72
  175.0 1.7 fusion.51
  176.9 1.1 copy.166
  178.8 2.4 copy.163
  181.2 1.1 copy.169
  183.5 178.7 %all-reduce.9.cloned.1.call-done = f32[192,3,768]{2,0,1:T(8,128)} async-done(((f32[192,3,768]{2,0,1:T(8,128)}), f32[192,3,768]{2,0,1:T(8,128)}) %all-reduce.9.cloned.1.call-update) | async-done | bytes 1769488 | tf_op jit(solution)/shard_map/psum | solution.py:84
  362.2 1.6 add_convert_fusion
  363.8 0.8 fusion.77
  365.3 0.7 fusion.37
  367.1 1.8 bitcast_reduce_fusion.1
  368.9 1.3 fusion.16
  370.2 0.9 bitcast_reduce_fusion
  371.7 1.1 copy-done.1
  372.9 1.8 fusion.2
  374.7 128.4 %pmax.14 = f32[96,6,2]{0,2,1:T(2,128)} all-reduce(f32[96,6,2]{0,2,1:T(2,128)} %max.21), channel_id=1, replica_groups=mesh['seq'=64,'mp'=8] {'seq'}, use_global_device_ids=true, to_apply=%region_12.13 | all-reduce | flops 1152 | bytes 9216 | tf_op jit(solution)/shard_map/pmax | solution.py:125
  503.0 1.4 add_multiply_fusion
  504.4 130.1 %psum.68 = f32[96,6,2]{0,2,1:T(2,128)} all-reduce(f32[96,6,2]{0,2,1:T(2,128)} %get-tuple-element.22), channel_id=1, replica_groups=mesh['seq'=64,'mp'=8] {'seq'}, use_global_device_ids=true, to_apply=%region_17.18 | all-reduce | flops 1152 | bytes 9216 | tf_op jit(solution)/shard_map/psum | solution.py:127
  634.5 3.3 fusion.18
  638.0 1.7 fusion.15
  641.4 184.1 %all-reduce.11.cloned.1.call-done = f32[96,6,2,128]{3,0,2,1:T(8,128)} async-done(((f32[96,6,2,128]{3,0,2,1:T(8,128)}), f32[96,6,2,128]{3,0,2,1:T(8,128)}) %all-reduce.11.cloned.1.call-update) | async-done | bytes 589840 | tf_op jit(solution)/shard_map/psum | solution.py:127
  825.5 1.7 fusion.34
  827.4 0.9 fusion.31
  828.4 74.0 %all-reduce.13.cloned.1.call-done = f32[192,112]{1,0:T(8,128)} async-done(((f32[192,112]{1,0:T(8,128)}), f32[192,112]{1,0:T(8,128)}) %all-reduce.13.cloned.1.call-update) | async-done | bytes 86032 | tf_op jit(solution)/shard_map/psum | solution.py:154
  902.4 1.0 fusion.72
  903.6 245.9 %all-reduce.2 = (f32[96,2]{1,0:T(8,128)S(1)}, f32[192]{0:T(256)S(1)}) all-reduce(f32[96,2]{1,0:T(8,128)S(1)} %reshape.242, f32[192]{0:T(256)S(1)} %get-tuple-element.5), channel_id=1, replica_groups=mesh['seq'=64,'mp'=8] {'seq'}, use_global_device_ids=true, to_apply=%region_21.22 | all-reduce | flops 384 | bytes 3072 | tf_op jit(solution)/shard_map/psum | solution.py:155
  1150.0 1.4 convolution_bitcast_fusion
  1154.3 246.3 %all-reduce = f32[6144]{0:T(1024)S(1)} all-reduce(f32[6144]{0:T(1024)S(1)} %dynamic-update-slice), channel_id=2, replica_groups=mesh['seq'=64,'mp'=8] {'seq'}, use_global_device_ids=true, to_apply=%add | all-reduce | flops 6144 | bytes 49152
  1401.8 1.1 dynamic-slice_reduce_fusion
  1402.8 97.9 %pmax.15 = f32[96]{0:T(128)} all-reduce(f32[96]{0:T(128)S(1)} %dynamic-slice_reduce_fusion), channel_id=1, replica_groups=mesh['seq'=64,'mp'=8] {'seq','mp'}, use_global_device_ids=true, to_apply=%region_27.28 | all-reduce | flops 96 | bytes 768 | tf_op jit(solution)/shard_map/pmax | solution.py:177
  (138 shorter events, 12.8 us)
Async XLA Ops:
  7.2 167.8 %copy-start = (bf16[112,3,768]{2,0,1:T(8,128)(2,1)S(1)}, bf16[112,3,768]{2,0,1:T(8,128)(2,1)}, u32[]{:S(2)}) copy-start(bf16[112,3,768]{2,0,1:T(8,128)(2,1)} %param.28) | copy-start | bytes 1548292
  7.2 35.1 %copy-start.33 = (bf16[2,112]{1,0:T(2,128)(2,1)S(1)}, bf16[2,112]{1,0:T(2,128)(2,1)}, u32[]{:S(2)}) copy-start(bf16[2,112]{1,0:T(2,128)(2,1)} %param.27) | copy-start | bytes 1348
  7.2 35.2 %copy-start.34 = (bf16[2,112]{1,0:T(2,128)(2,1)S(1)}, bf16[2,112]{1,0:T(2,128)(2,1)}, u32[]{:S(2)}) copy-start(bf16[2,112]{1,0:T(2,128)(2,1)} %param.26) | copy-start | bytes 1348
  7.2 355.0 %all-reduce.9.cloned.1.call-start = ((), (), s32[]{:S(2)}) async-start(), calls=%async_computation | async-start | bytes 3538944 | tf_op jit(solution)/shard_map/psum | solution.py:84
  42.3 134.4 %copy-start.8 = (bf16[192,112]{1,0:T(8,128)(2,1)}, bf16[192,112]{1,0:T(8,128)(2,1)S(1)}, u32[]{:S(2)}) copy-start(bf16[192,112]{1,0:T(8,128)(2,1)S(1)} %psum.63) | copy-start | bytes 129028
  176.7 648.8 %all-reduce.11.cloned.1.call-start = ((), (), s32[]{:S(2)}) async-start(), calls=%async_computation.1 | async-start | bytes 1179648 | tf_op jit(solution)/shard_map/psum | solution.py:127
  178.2 3.1 copy-start.11
  178.8 3.5 copy-start.27
  178.8 3.6 copy-start.30
  178.8 3.7 copy-start.31
  366.3 2.6 copy-start.13
  367.1 3.1 copy-start.4
  372.9 261.7 %copy-start.6 = (bf16[768,768]{0,1:T(8,128)(2,1)S(1)}, bf16[768,768]{0,1:T(8,128)(2,1)}, u32[]{:S(2)}) copy-start(bf16[768,768]{0,1:T(8,128)(2,1)} %copy.163) | copy-start | bytes 3538948
  634.5 3.3 copy-start.12
  634.5 3.3 copy-start.14
  634.5 3.3 copy-start.23
  634.5 3.4 copy-start.24
  637.9 2.0 copy-start.17
  637.9 2.0 copy-start.18
  637.9 2.0 copy-start.20
  637.9 2.0 copy-start.21
  637.9 2.3 copy-start.7
  639.6 262.7 %all-reduce.13.cloned.1.call-start = ((), (), s32[]{:S(2)}) async-start(), calls=%async_computation.2 | async-start | bytes 196608 | tf_op jit(solution)/shard_map/psum | solution.py:154
  640.6 186.8 %copy-start.15 = (bf16[768,112]{0,1:T(8,128)(2,1)S(1)}, bf16[768,112]{0,1:T(8,128)(2,1)}, u32[]{:S(2)}) copy-start(bf16[768,112]{0,1:T(8,128)(2,1)} %param.30) | copy-start | bytes 516100
  641.3 187.0 %copy-start.35 = (bf16[112]{0:T(256)(128)(2,1)S(1)}, bf16[112]{0:T(256)(128)(2,1)}, u32[]{:S(2)}) copy-start(bf16[112]{0:T(256)(128)(2,1)} %param.31) | copy-start | bytes 676
  641.3 261.0 %copy-start.9 = (bf16[192,112]{1,0:T(8,128)(2,1)S(1)}, bf16[192,112]{1,0:T(8,128)(2,1)}, u32[]{:S(2)}) copy-start(bf16[192,112]{1,0:T(8,128)(2,1)} %copy-done.8) | copy-start | bytes 129028
  641.4 508.5 %copy-start.25 = (f32[112]{0:T(128)S(1)}, f32[112]{0:T(128)}, u32[]{:S(2)}) copy-start(f32[112]{0:T(128)} %get-tuple-element.33) | copy-start | bytes 1348
  641.4 508.5 %copy-start.26 = (f32[112]{0:T(128)S(1)}, f32[112]{0:T(128)}, u32[]{:S(2)}) copy-start(f32[112]{0:T(128)} %get-tuple-element.42) | copy-start | bytes 1348
  825.5 324.5 %copy-start.2 = (bf16[3200,112]{0,1:T(8,128)(2,1)S(1)}, bf16[3200,112]{0,1:T(8,128)(2,1)}, u32[]{:S(2)}) copy-start(bf16[3200,112]{0,1:T(8,128)(2,1)} %param.32) | copy-start | bytes 2150404
  828.3 573.5 %all-reduce.15.cloned.1.call-start = ((), (), s32[]{:S(2)}) async-start(), calls=%async_computation.3 | async-start | bytes 2457600
  903.6 247.8 %copy-start.28 = (u32[512]{0:T(512)S(1)}, u32[512]{0:T(512)}, u32[]{:S(2)}) copy-start(u32[512]{0:T(512)} %constant.73) | copy-start | bytes 6148
  1149.7 4.3 copy-start.32
  (8 other events, 12.7 us)
Sparse Core Ops, SparseCore 0:
  176.8 185.3 all-reduce.8
  639.8 185.7 all-reduce.10
  828.4 73.9 all-reduce.12
  1151.5 191.1 all-reduce.14
